TPU v7x, 32 devices: a whole 2x2x4 slice. The times are simulated.
32 devices in a mesh: groups: 2 (over y), wide: 4 (over z), narrow: 4 (over x, core).
Axes of the slice: x: 2, y: 2, z: 4, core: 2. Of those that a mesh axis runs over, the one named last changes fastest.
Arguments:
- tiles: bfloat16 [8, 4, 224, 128, 128], P(('groups', 'wide'), 'narrow'), parts along dimension 0, may hold values from 0.19921875 to 20
- tile_rows: int32 [8, 4, 224], P(('groups', 'wide'), 'narrow'), parts along dimension 0, may hold values from 0 to 15, as said below
- tile_cols: int32 [8, 4, 224], P(('groups', 'wide'), 'narrow'), parts along dimension 0, may hold values from 0 to 31
- tile_live: int32 [8, 4, 224], P(('groups', 'wide'), 'narrow'), parts along dimension 0, may hold values 0 or 1
- omega: bfloat16 [32768, 256], P(('groups', 'narrow')), parts along dimension 0, may hold values from -0.0625 to 0.0625
- psi: bfloat16 [512, 16384], P(None, ('groups', 'wide')), parts along dimension 1, may hold values from -0.09375 to 0.09375
Outputs:
- range_sketch: float32 [16384, 256], P(('groups', 'wide', 'narrow')), parts along dimension 0
- corange_sketch: float32 [512, 32768], P('wide', ('groups', 'narrow')), parts along dimension 1
There are 2 independent parts, one for each index of `groups`. A program takes and returns all parts, laid end to end along the dimension named above; each array names one. Nothing has to cross between parts.
Inputs may be any that keep to these rules, and one draw needn't show every extreme that they name: Within one device's slots no two slots share the same pair (tile_rows, tile_cols).
All inputs are finite; a program needn't handle non-finite values. No bound on the sum of `tile_live` on one device may be relied on, other than what follows from the above.
Results may differ from a plain program's by a relative error of at most 0.005.
Values sent between devices are 32-bit elements; how exact they have to be, the bound alone decides.
A program may use at most 128 MiB of HBM per device.

v0:
```python
import jax
import jax.numpy as jnp
from jax import lax
from jax.sharding import PartitionSpec as P


def on_device(tiles, tile_rows, tile_cols, tile_live, omega, psi):
    slots = tiles.shape[2]
    tile = tiles.shape[3]
    rank = omega.shape[1]
    corank = psi.shape[0]
    row_blocks = psi.shape[1] // tile
    col_blocks = omega.shape[0] // tile
    step = max([size for size in range(1, 33) if slots % size == 0])
    groups_count = slots // step
    values = jnp.log(jnp.maximum(tiles.reshape(slots, tile, tile).astype(jnp.float32), 1.0)).astype(
        jnp.bfloat16
    )
    livef = tile_live.reshape(slots).astype(jnp.float32)
    rows = tile_rows.reshape(slots)
    cols = tile_cols.reshape(slots)
    pick_rows = (rows[:, None] == jnp.arange(row_blocks, dtype=jnp.int32)[None, :]).astype(
        jnp.float32
    ) * livef[:, None]
    pick_cols = (cols[:, None] == jnp.arange(col_blocks, dtype=jnp.int32)[None, :]).astype(
        jnp.float32
    ) * livef[:, None]
    grouped = values.reshape(groups_count, step, tile, tile)
    rows_g = rows.reshape(groups_count, step)
    cols_g = cols.reshape(groups_count, step)
    prow_g = pick_rows.reshape(groups_count, step, row_blocks)
    pcol_g = pick_cols.reshape(groups_count, step, col_blocks)
    omega_blocks = omega.reshape(col_blocks, tile, rank)

    def range_visit(acc, block):
        vals, cidx, prow = block
        picked = jnp.take(omega_blocks, cidx, axis=0)
        prod = jnp.einsum("sij,sjk->sik", vals, picked, preferred_element_type=jnp.float32)
        return (acc + jnp.einsum("sr,sik->rik", prow, prod), None)

    acc, _ = lax.scan(
        range_visit, jnp.zeros((row_blocks, tile, rank), jnp.float32), (grouped, cols_g, prow_g)
    )
    range_sketch = lax.psum_scatter(
        acc.reshape(row_blocks * tile, rank), "narrow", scatter_dimension=0, tiled=True
    )
    share = corank // lax.axis_size("wide")
    blocks = psi.reshape(corank, row_blocks, tile).transpose(1, 0, 2)

    def corange_visit(acc, block):
        vals, ridx, pcol = block
        picked = jnp.take(blocks, ridx, axis=0)
        prod = jnp.einsum("sli,sij->slj", picked, vals, preferred_element_type=jnp.float32)
        return (acc + jnp.einsum("sc,slj->clj", pcol, prod), None)

    acc, _ = lax.scan(
        corange_visit, jnp.zeros((col_blocks, corank, tile), jnp.float32), (grouped, rows_g, pcol_g)
    )
    summed = lax.psum(acc.transpose(1, 0, 2).reshape(corank, col_blocks * tile), "wide")
    corange_sketch = lax.dynamic_slice_in_dim(summed, lax.axis_index("wide") * share, share, 0)
    return (range_sketch, corange_sketch)


def solution(mesh):
    in_specs = (
        P(("groups", "wide"), "narrow", None, None, None),
        P(("groups", "wide"), "narrow", None),
        P(("groups", "wide"), "narrow", None),
        P(("groups", "wide"), "narrow", None),
        P(("groups", "narrow"), None),
        P(None, ("groups", "wide")),
    )
    out_specs = (P(("groups", "wide", "narrow"), None), P("wide", ("groups", "narrow")))
    return jax.shard_map(
        on_device, mesh=mesh, in_specs=in_specs, out_specs=out_specs, check_vma=False
    )
```

profile of v0, /device:TPU:16, one launch (start us, length us, event | category | flops | bytes accessed | tf_op | source)
XLA Modules:
  0.0 479.2 jit_solution(2181536055452326515)
XLA Ops:
  12.2 9.7 %log_convert_fusion = bf16[1,1,224,128,128]{4,3,2,1,0:T(8,128)(2,1)} fusion(bf16[1,1,224,128,128]{4,3,2,1,0:T(8,128)(2,1)} %param.10), kind=kLoop, calls=%fused_computation.42 | loop fusion | flops 11010048 | bytes 14680064 | tf_op jit(solution)/shard_map/convert_element_type | solution.py:16
  27.5 135.4 %while.23 = (s32[]{:T(128)}, f32[32,512,128]{2,0,1:T(8,128)}, bf16[7,32,32]{1,2,0:T(8,128)(2,1)S(1)}, s32[7,32]{1,0:T(8,128)S(1)}, bf16[16,512,128]{2,1,0:T(8,12...) while((s32[]{:T(128)}, f32[32,512,128]{2,0,1:T(8,128)}, ...), condition=%wide.region_4.5_spmd.clone, body=%wide.region_3.4_spmd.clone.sunk | while | flops 677381440 | bytes 38810920 | solution.py:56
  30.6 5.7 %fusion.57 = bf16[32,512,128]{2,1,0:T(8,128)(2,1)} fusion(bf16[32,512,128]{2,1,0:T(8,128)(2,1)} %gather_fusion.1, pred[32]{0:T(512)(128)(4,1)S(1)} %compare_and_fusion.5, bf16[7,32,128,128]{3,2,1,0:T(8,128)(2,1)} %get-tuple-element.259, s32[]{:T(128)} %get-tuple-element.246), kind=kOutput, calls=%fused_computation.25.clone.1 | convolution fusion | flops 538968064 | bytes 9437728 | tf_op jit(solution)/shard_map/while/body/eval_jaxpr/sli,sij->slj/dot_general | solution.py:53
  36.3 8.4 %select_add_fusion.5 = f32[32,512,128]{2,0,1:T(8,128)} fusion(f32[32,512,128]{2,0,1:T(8,128)} %get-tuple-element.247, pred[]{:T(512)S(6)} %compare.7, bf16[32,512,128]{2,1,0:T(8,128)(2,1)} %fusion.57, bf16[7,32,32]{1,2,0:T(8,128)(2,1)S(1)} %get-tuple-element.256, s32[]{:T(128)} %get-tuple-element.246), kind=kOutput, calls=%fused_computation.24.clone.1 | convolution fusion | flops 138412032 | bytes 20979716 | tf_op jit(solution)/shard_map/while/body/eval_jaxpr/sc,slj->clj/dot_general | solution.py:54
  47.8 5.7 %fusion.57 = bf16[32,512,128]{2,1,0:T(8,128)(2,1)} fusion(bf16[32,512,128]{2,1,0:T(8,128)(2,1)} %gather_fusion.1, pred[32]{0:T(512)(128)(4,1)S(1)} %compare_and_fusion.5, bf16[7,32,128,128]{3,2,1,0:T(8,128)(2,1)} %get-tuple-element.259, s32[]{:T(128)} %get-tuple-element.246), kind=kOutput, calls=%fused_computation.25.clone.1 | convolution fusion | flops 538968064 | bytes 9437728 | tf_op jit(solution)/shard_map/while/body/eval_jaxpr/sli,sij->slj/dot_general | solution.py:53
  53.5 10.9 %select_add_fusion.5 = f32[32,512,128]{2,0,1:T(8,128)} fusion(f32[32,512,128]{2,0,1:T(8,128)} %get-tuple-element.247, pred[]{:T(512)S(6)} %compare.7, bf16[32,512,128]{2,1,0:T(8,128)(2,1)} %fusion.57, bf16[7,32,32]{1,2,0:T(8,128)(2,1)S(1)} %get-tuple-element.256, s32[]{:T(128)} %get-tuple-element.246), kind=kOutput, calls=%fused_computation.24.clone.1 | convolution fusion | flops 138412032 | bytes 20979716 | tf_op jit(solution)/shard_map/while/body/eval_jaxpr/sc,slj->clj/dot_general | solution.py:54
  67.5 5.7 %fusion.57 = bf16[32,512,128]{2,1,0:T(8,128)(2,1)} fusion(bf16[32,512,128]{2,1,0:T(8,128)(2,1)} %gather_fusion.1, pred[32]{0:T(512)(128)(4,1)S(1)} %compare_and_fusion.5, bf16[7,32,128,128]{3,2,1,0:T(8,128)(2,1)} %get-tuple-element.259, s32[]{:T(128)} %get-tuple-element.246), kind=kOutput, calls=%fused_computation.25.clone.1 | convolution fusion | flops 538968064 | bytes 9437728 | tf_op jit(solution)/shard_map/while/body/eval_jaxpr/sli,sij->slj/dot_general | solution.py:53
  73.2 10.9 %select_add_fusion.5 = f32[32,512,128]{2,0,1:T(8,128)} fusion(f32[32,512,128]{2,0,1:T(8,128)} %get-tuple-element.247, pred[]{:T(512)S(6)} %compare.7, bf16[32,512,128]{2,1,0:T(8,128)(2,1)} %fusion.57, bf16[7,32,32]{1,2,0:T(8,128)(2,1)S(1)} %get-tuple-element.256, s32[]{:T(128)} %get-tuple-element.246), kind=kOutput, calls=%fused_computation.24.clone.1 | convolution fusion | flops 138412032 | bytes 20979716 | tf_op jit(solution)/shard_map/while/body/eval_jaxpr/sc,slj->clj/dot_general | solution.py:54
  87.2 5.7 %fusion.57 = bf16[32,512,128]{2,1,0:T(8,128)(2,1)} fusion(bf16[32,512,128]{2,1,0:T(8,128)(2,1)} %gather_fusion.1, pred[32]{0:T(512)(128)(4,1)S(1)} %compare_and_fusion.5, bf16[7,32,128,128]{3,2,1,0:T(8,128)(2,1)} %get-tuple-element.259, s32[]{:T(128)} %get-tuple-element.246), kind=kOutput, calls=%fused_computation.25.clone.1 | convolution fusion | flops 538968064 | bytes 9437728 | tf_op jit(solution)/shard_map/while/body/eval_jaxpr/sli,sij->slj/dot_general | solution.py:53
  92.9 10.9 %select_add_fusion.5 = f32[32,512,128]{2,0,1:T(8,128)} fusion(f32[32,512,128]{2,0,1:T(8,128)} %get-tuple-element.247, pred[]{:T(512)S(6)} %compare.7, bf16[32,512,128]{2,1,0:T(8,128)(2,1)} %fusion.57, bf16[7,32,32]{1,2,0:T(8,128)(2,1)S(1)} %get-tuple-element.256, s32[]{:T(128)} %get-tuple-element.246), kind=kOutput, calls=%fused_computation.24.clone.1 | convolution fusion | flops 138412032 | bytes 20979716 | tf_op jit(solution)/shard_map/while/body/eval_jaxpr/sc,slj->clj/dot_general | solution.py:54
  106.9 5.7 %fusion.57 = bf16[32,512,128]{2,1,0:T(8,128)(2,1)} fusion(bf16[32,512,128]{2,1,0:T(8,128)(2,1)} %gather_fusion.1, pred[32]{0:T(512)(128)(4,1)S(1)} %compare_and_fusion.5, bf16[7,32,128,128]{3,2,1,0:T(8,128)(2,1)} %get-tuple-element.259, s32[]{:T(128)} %get-tuple-element.246), kind=kOutput, calls=%fused_computation.25.clone.1 | convolution fusion | flops 538968064 | bytes 9437728 | tf_op jit(solution)/shard_map/while/body/eval_jaxpr/sli,sij->slj/dot_general | solution.py:53
  112.6 10.9 %select_add_fusion.5 = f32[32,512,128]{2,0,1:T(8,128)} fusion(f32[32,512,128]{2,0,1:T(8,128)} %get-tuple-element.247, pred[]{:T(512)S(6)} %compare.7, bf16[32,512,128]{2,1,0:T(8,128)(2,1)} %fusion.57, bf16[7,32,32]{1,2,0:T(8,128)(2,1)S(1)} %get-tuple-element.256, s32[]{:T(128)} %get-tuple-element.246), kind=kOutput, calls=%fused_computation.24.clone.1 | convolution fusion | flops 138412032 | bytes 20979716 | tf_op jit(solution)/shard_map/while/body/eval_jaxpr/sc,slj->clj/dot_general | solution.py:54
  126.6 5.7 %fusion.57 = bf16[32,512,128]{2,1,0:T(8,128)(2,1)} fusion(bf16[32,512,128]{2,1,0:T(8,128)(2,1)} %gather_fusion.1, pred[32]{0:T(512)(128)(4,1)S(1)} %compare_and_fusion.5, bf16[7,32,128,128]{3,2,1,0:T(8,128)(2,1)} %get-tuple-element.259, s32[]{:T(128)} %get-tuple-element.246), kind=kOutput, calls=%fused_computation.25.clone.1 | convolution fusion | flops 538968064 | bytes 9437728 | tf_op jit(solution)/shard_map/while/body/eval_jaxpr/sli,sij->slj/dot_general | solution.py:53
  132.3 10.9 %select_add_fusion.5 = f32[32,512,128]{2,0,1:T(8,128)} fusion(f32[32,512,128]{2,0,1:T(8,128)} %get-tuple-element.247, pred[]{:T(512)S(6)} %compare.7, bf16[32,512,128]{2,1,0:T(8,128)(2,1)} %fusion.57, bf16[7,32,32]{1,2,0:T(8,128)(2,1)S(1)} %get-tuple-element.256, s32[]{:T(128)} %get-tuple-element.246), kind=kOutput, calls=%fused_computation.24.clone.1 | convolution fusion | flops 138412032 | bytes 20979716 | tf_op jit(solution)/shard_map/while/body/eval_jaxpr/sc,slj->clj/dot_general | solution.py:54
  146.3 5.7 %fusion.57 = bf16[32,512,128]{2,1,0:T(8,128)(2,1)} fusion(bf16[32,512,128]{2,1,0:T(8,128)(2,1)} %gather_fusion.1, pred[32]{0:T(512)(128)(4,1)S(1)} %compare_and_fusion.5, bf16[7,32,128,128]{3,2,1,0:T(8,128)(2,1)} %get-tuple-element.259, s32[]{:T(128)} %get-tuple-element.246), kind=kOutput, calls=%fused_computation.25.clone.1 | convolution fusion | flops 538968064 | bytes 9437728 | tf_op jit(solution)/shard_map/while/body/eval_jaxpr/sli,sij->slj/dot_general | solution.py:53
  152.0 10.9 %select_add_fusion.5 = f32[32,512,128]{2,0,1:T(8,128)} fusion(f32[32,512,128]{2,0,1:T(8,128)} %get-tuple-element.247, pred[]{:T(512)S(6)} %compare.7, bf16[32,512,128]{2,1,0:T(8,128)(2,1)} %fusion.57, bf16[7,32,32]{1,2,0:T(8,128)(2,1)S(1)} %get-tuple-element.256, s32[]{:T(128)} %get-tuple-element.246), kind=kOutput, calls=%fused_computation.24.clone.1 | convolution fusion | flops 138412032 | bytes 20979716 | tf_op jit(solution)/shard_map/while/body/eval_jaxpr/sc,slj->clj/dot_general | solution.py:54
  162.9 14.7 %copy.24 = f32[64,8,32,128]{3,1,2,0:T(8,128)} copy(f32[64,8,32,128]{3,2,1,0:T(8,128)} %bitcast.57) | data formatting | bytes 16777216
  177.7 73.6 %while.22 = (s32[]{:T(128)}, f32[16,128,256]{2,0,1:T(8,128)}, bf16[7,32,16]{1,2,0:T(8,128)(2,1)S(1)}, bf16[7,32,128,128]{3,2,1,0:T(8,128)(2,1)}, s32[7,32]{1,0:T...) while((s32[]{:T(128)}, f32[16,128,256]{2,0,1:T(8,128)}, ...), condition=%wide.region_1.2_spmd.clone, body=%wide.region_0.1_spmd.clone.sunk | while | flops 304088352 | bytes 15738155 | solution.py:41
  177.9 3.7 gather_fusion
  187.0 3.7 gather_fusion
  193.4 4.3 select_add_fusion.4
  197.7 3.7 gather_fusion
  204.1 4.3 select_add_fusion.4
  208.4 3.7 gather_fusion
  214.9 4.3 select_add_fusion.4
  219.1 3.7 gather_fusion
  225.5 4.3 select_add_fusion.4
  229.8 3.7 gather_fusion
  236.3 4.3 select_add_fusion.4
  247.0 4.3 select_add_fusion.4
  251.3 4.2 copy.9
  255.5 213.2 %all-reduce.2.cloned.1.call-done = f32[512,4096]{1,0:T(8,128)} async-done(((f32[512,4096]{1,0:T(8,128)}), f32[512,4096]{1,0:T(8,128)}) %all-reduce.2.cloned.1.call-update) | async-done | bytes 8388624 | tf_op jit(solution)/shard_map/psum | solution.py:59
  (79 shorter events, 60.0 us)
Async XLA Ops:
  8.0 460.7 %all-reduce.2.cloned.1.call-start = ((), (), s32[]{:S(2)}) async-start(), calls=%async_computation.2 | async-start | bytes 16777216 | tf_op jit(solution)/shard_map/psum | solution.py:59
  12.2 9.7 %copy-start = (bf16[512,2048]{1,0:T(8,128)(2,1)S(1)}, bf16[512,2048]{1,0:T(8,128)(2,1)}, u32[]{:S(2)}) copy-start(bf16[512,2048]{1,0:T(8,128)(2,1)} %param.15) | copy-start | bytes 6291460
  177.6 294.2 %reduce-scatter.2.cloned.1.call-start = ((), (), s32[]{:S(2)}) async-start(), calls=%async_computation.1 | async-start | bytes 2621440 | tf_op jit(solution)/shard_map/reduce_scatter | solution.py:44
Sparse Core Ops, SparseCore 0:
  177.7 290.9 all-reduce.1
Sparse Core Ops, SparseCore 1:
  255.5 32.4 reduce-scatter.1
where the time goes:
time: 483 us; the launch traced here: 479 us
  waiting for transfers between devices  213 us (44%)
  matrix products  161 us (33%)
  local copies, waits for them, and re-layouts  75.3 us (16%)
  between operations  15.5 us (3%)
  other arithmetic  13.5 us (3%)
    psum x1, waiting for transfers between devices, on_device(): lax.psum(acc.transpose(1, 0, 2).reshape(corank, col_blocks * tile), 'wide')  213 us
    dot_general x7, matrix products, corange_visit(): return (acc + jnp.einsum('sc,slj->clj', pcol, prod), None)  73.8 us
    dot_general x7, matrix products, corange_visit(): jnp.einsum('sli,sij->slj', picked, vals, preferred_element_type=jnp.float32)  40 us
    dot_general x7, matrix products, range_visit(): return (acc + jnp.einsum('sr,sik->rik', prow, prod), None)  28.3 us
    gather x7, local copies, waits for them, and re-layouts, range_visit(): picked = jnp.take(omega_blocks, cidx, axis=0)  25.7 us
    gather x7, local copies, waits for them, and re-layouts, corange_visit(): picked = jnp.take(blocks, ridx, axis=0)  21.4 us
    unnamed x6, local copies, waits for them, and re-layouts  20.7 us
    dot_general x7, matrix products, range_visit(): jnp.einsum('sij,sjk->sik', vals, picked, preferred_element_type=jnp.float32)  19 us
  transfers between devices with their start and end apart: 2, of which 1 were waited for; matrix products, arithmetic and copies ran while one was open for 17% of the time, Pallas kernels for 0%

commit v1 on v0

v1 whole, which is shorter than its diff:
```python
import functools

import jax
import jax.numpy as jnp
from jax import lax
from jax.experimental import pallas as pl
from jax.experimental.pallas import tpu as pltpu
from jax.sharding import PartitionSpec as P

MESH = pl.DeviceIdType.MESH
F32 = jnp.float32
BF16 = jnp.bfloat16


def kernel(
    nw, nn, width, depth,
    slot_at, tiles_hbm, psi_hbm, omega_hbm, range_hbm, corange_hbm,
    tiles, psi, omega, dense, part, arrived, rpart, rarrived,
    in_sem, send_sem, recv_sem, rsend_sem, rrecv_sem, out_sem, rout_sem,
):
    me = lax.axis_index("wide")
    mine = lax.axis_index("narrow")
    slots, tile = tiles_hbm.shape[0], tiles_hbm.shape[1]
    corank, rows = psi.shape
    chunks = part.shape[0]
    share = corank // nw
    rblock = rows // nn
    row_blocks = rows // tile
    per_chunk = width // tile

    in_copies = [
        pltpu.make_async_copy(tiles_hbm, tiles.at[pl.ds(0, slots)], in_sem.at[0]),
        pltpu.make_async_copy(psi_hbm, psi, in_sem.at[1]),
        pltpu.make_async_copy(omega_hbm, omega, in_sem.at[2]),
    ]
    for copy in in_copies:
        copy.start()

    barrier = pltpu.get_barrier_semaphore()

    @pl.when(me > 0)
    def _():
        pl.semaphore_signal(barrier, inc=1, device_id={"wide": me - 1}, device_id_type=MESH)

    @pl.when(me < nw - 1)
    def _():
        pl.semaphore_signal(barrier, inc=1, device_id={"wide": me + 1}, device_id_type=MESH)

    for d in range(1, nn):
        pl.semaphore_signal(
            barrier, inc=1, device_id={"narrow": lax.rem(mine + d, nn)}, device_id_type=MESH
        )
    tiles[slots] = jnp.ones((tile, tile), BF16)
    rpart[...] = jnp.zeros_like(rpart)
    near = jnp.where(me > 0, 1, 0) + jnp.where(me < nw - 1, 1, 0)
    pl.semaphore_wait(barrier, nn - 1 + near)

    def own(j, c):
        return part.at[c, pl.ds(pl.multiple_of(j * share, share), share)]

    def rightward(j, c):
        return pltpu.make_async_remote_copy(
            src_ref=own(j, c), dst_ref=arrived.at[j, c],
            send_sem=send_sem.at[j, c], recv_sem=recv_sem.at[j, c],
            device_id={"wide": me + 1}, device_id_type=MESH,
        )

    def leftward(j, c):
        slot = jnp.where(j == me - 1, nw, j)
        return pltpu.make_async_remote_copy(
            src_ref=own(j, c), dst_ref=arrived.at[slot, c],
            send_sem=send_sem.at[j, c], recv_sem=recv_sem.at[slot, c],
            device_id={"wide": me - 1}, device_id_type=MESH,
        )

    def await_arrival(slot, c):
        pltpu.make_async_copy(arrived.at[slot, c], arrived.at[slot, c], recv_sem.at[slot, c]).wait()

    def add_arrived(j, slot, c):
        at = pl.ds(pl.multiple_of(j * share, share), share)
        part[c, at, :] = part[c, at, :] + arrived[slot, c]

    in_copies[0].wait()
    in_copies[1].wait()
    in_copies[2].wait()

    def chunk_step(c, carry):
        def place(r, carry):
            for q in range(per_chunk):
                value = tiles[slot_at[(c * per_chunk + q) * row_blocks + r]]
                value = jnp.log(jnp.maximum(value.astype(F32), 1.0)).astype(BF16)
                dense[pl.ds(pl.multiple_of(r * tile, tile), tile), q * tile : (q + 1) * tile] = value
            return carry

        lax.fori_loop(0, row_blocks, place, 0)

        def corange_rows(m, carry):
            at = pl.ds(pl.multiple_of(m * depth, depth), depth)
            part[c, at, :] = jnp.dot(psi[at, :], dense[...], preferred_element_type=F32)
            return carry

        lax.fori_loop(0, corank // depth, corange_rows, 0)

        @pl.when(me == 0)
        def _():
            rightward(nw - 1, c).start()

        @pl.when(me == nw - 1)
        def _():
            leftward(0, c).start()

        chosen = omega[pl.ds(pl.multiple_of(c * width, width), width), :]

        def range_rows(m, carry):
            at = pl.ds(pl.multiple_of(m * depth, depth), depth)
            rpart[at, :] = rpart[at, :] + jnp.dot(dense[at, :], chosen, preferred_element_type=F32)
            return carry

        lax.fori_loop(0, rows // depth, range_rows, 0)
        return carry

    lax.fori_loop(0, chunks, chunk_step, 0)

    def range_copy(d):
        to = lax.rem(mine + d, nn)
        return pltpu.make_async_remote_copy(
            src_ref=rpart.at[pl.ds(pl.multiple_of(to * rblock, rblock), rblock)],
            dst_ref=rarrived.at[d - 1],
            send_sem=rsend_sem.at[d - 1], recv_sem=rrecv_sem.at[d - 1],
            device_id={"narrow": to}, device_id_type=MESH,
        )

    for d in range(1, nn):
        range_copy(d).start()

    def line_step(k, carry):
        s, c = k // chunks, k % chunks
        right_share = nw - 1 - s
        left_share = s

        @pl.when(jnp.logical_and(me < right_share, jnp.logical_or(me > 0, s > 0)))
        def _():
            @pl.when(me > 0)
            def _():
                await_arrival(right_share, c)
                add_arrived(right_share, right_share, c)

            rightward(right_share, c).start()

        @pl.when(jnp.logical_and(me > left_share, jnp.logical_or(me < nw - 1, s > 0)))
        def _():
            @pl.when(me < nw - 1)
            def _():
                await_arrival(left_share, c)
                add_arrived(left_share, left_share, c)

            leftward(left_share, c).start()

        return carry

    lax.fori_loop(0, (nw - 1) * chunks, line_step, 0)

    at = pl.ds(pl.multiple_of(mine * rblock, rblock), rblock)
    for d in range(1, nn):
        range_copy(d).wait_recv()
    total = rpart[at, :]
    for d in range(1, nn):
        total = total + rarrived[d - 1]
    rpart[at, :] = total
    range_out = pltpu.make_async_copy(rpart.at[at], range_hbm, rout_sem)
    range_out.start()

    def share_out(c):
        return pltpu.make_async_copy(
            own(me, c), corange_hbm.at[:, pl.ds(pl.multiple_of(c * width, width), width)], out_sem.at[c]
        )

    def finish(c, carry):
        @pl.when(me < nw - 1)
        def _():
            await_arrival(nw, c)
            add_arrived(me, nw, c)

        @pl.when(me > 0)
        def _():
            await_arrival(me, c)
            add_arrived(me, me, c)

        share_out(c).start()
        return carry

    lax.fori_loop(0, chunks, finish, 0)

    def drain(k, carry):
        j, c = k // chunks, k % chunks

        @pl.when(j != me)
        def _():
            pltpu.make_async_copy(own(j, c), own(j, c), send_sem.at[j, c]).wait()

        return carry

    lax.fori_loop(0, nw * chunks, drain, 0)

    def drain_out(c, carry):
        share_out(c).wait()
        return carry

    lax.fori_loop(0, chunks, drain_out, 0)
    for d in range(1, nn):
        range_copy(d).wait_send()
    range_out.wait()


def on_device(nw, nn, tiles, tile_rows, tile_cols, tile_live, omega, psi):
    slots, tile = tiles.shape[2], tiles.shape[3]
    rank, corank = omega.shape[1], psi.shape[0]
    rows, cols = psi.shape[1], omega.shape[0]
    row_blocks, col_blocks = rows // tile, cols // tile
    width = 2 * tile
    depth = 2 * tile
    chunks = cols // width
    share, rblock = corank // nw, rows // nn

    place = jnp.where(tile_live > 0, tile_cols * row_blocks + tile_rows, -1).reshape(slots)
    hit = place[None, :] == jnp.arange(row_blocks * col_blocks, dtype=jnp.int32)[:, None]
    back = jnp.arange(slots, dtype=jnp.int32) - slots
    slot_at = slots + jnp.sum(jnp.where(hit, back[None, :], 0), axis=1, dtype=jnp.int32)

    return pl.pallas_call(
        functools.partial(kernel, nw, nn, width, depth),
        out_shape=(
            jax.ShapeDtypeStruct((rblock, rank), F32),
            jax.ShapeDtypeStruct((share, cols), F32),
        ),
        in_specs=[pl.BlockSpec(memory_space=pltpu.SMEM)] + [pl.BlockSpec(memory_space=pl.ANY)] * 3,
        out_specs=(pl.BlockSpec(memory_space=pl.ANY),) * 2,
        scratch_shapes=[
            pltpu.VMEM((slots + 1, tile, tile), BF16),
            pltpu.VMEM((corank, rows), BF16),
            pltpu.VMEM((cols, rank), BF16),
            pltpu.VMEM((rows, width), BF16),
            pltpu.VMEM((chunks, corank, width), F32),
            pltpu.VMEM((nw + 1, chunks, share, width), F32),
            pltpu.VMEM((rows, rank), F32),
            pltpu.VMEM((nn - 1, rblock, rank), F32),
            pltpu.SemaphoreType.DMA((3,)),
            pltpu.SemaphoreType.DMA((nw, chunks)),
            pltpu.SemaphoreType.DMA((nw + 1, chunks)),
            pltpu.SemaphoreType.DMA((nn - 1,)),
            pltpu.SemaphoreType.DMA((nn - 1,)),
            pltpu.SemaphoreType.DMA((chunks,)),
            pltpu.SemaphoreType.DMA,
        ],
        compiler_params=pltpu.CompilerParams(
            collective_id=0, has_side_effects=True, vmem_limit_bytes=52 << 20
        ),
        name="sketch",
    )(slot_at, tiles.reshape(slots, tile, tile), psi, omega)


def solution(mesh):
    in_specs = (
        P(("groups", "wide"), "narrow", None, None, None),
        P(("groups", "wide"), "narrow", None),
        P(("groups", "wide"), "narrow", None),
        P(("groups", "wide"), "narrow", None),
        P(("groups", "narrow"), None),
        P(None, ("groups", "wide")),
    )
    out_specs = (P(("groups", "wide", "narrow"), None), P("wide", ("groups", "narrow")))
    return jax.shard_map(
        functools.partial(on_device, mesh.shape["wide"], mesh.shape["narrow"]),
        mesh=mesh, in_specs=in_specs, out_specs=out_specs, check_vma=False,
    )
```

time: 483 us -> 227 us (0.47)
  Pallas kernels: 0 us -> 222 us
  waiting for transfers between devices: 213 us -> 0 us
  matrix products: 161 us -> 0 us
  local copies, waits for them, and re-layouts: 75.3 us -> 3.91 us
  between operations: 15.5 us -> 0.64 us
  other arithmetic: 13.5 us -> 0.87 us
    pallas_call x0 -> x1, Pallas kernels: none -> 222 us  [on_device(): pl.pallas_call(functools.partial(kernel, nw, nn, width, depth), out_shape...]
    psum x1 -> x0, waiting for transfers between devices: 213 us -> none  [on_device(): lax.psum(acc.transpose(1, 0, 2).reshape(corank, col_blocks * tile), 'wide')]
    dot_general x28 -> x0, matrix products: 161 us -> none  [the longest x7 73.8 us: corange_visit(): return (acc + jnp.einsum('sc,slj->clj', pcol, prod), None)]
    gather x14 -> x0, local copies, waits for them, and re-layouts: 47.1 us -> none  [the longest x7 25.7 us: range_visit(): picked = jnp.take(omega_blocks, cidx, axis=0)]
    unnamed x6 -> x2, local copies, waits for them, and re-layouts: 20.7 us -> 3.91 us
    convert_element_type x2 -> x0, other arithmetic: 10.4 us -> none  [the longest x1 9.72 us: on_device(): jnp.log(jnp.maximum(tiles.reshape(slots, tile, tile).astype(jnp.float32),...]
  transfers between devices with their start and end apart: 2 -> 0, of which waited for: 1 -> 0; matrix products, arithmetic and copies ran while one was open for 17% -> 0% of each run, Pallas kernels for 0% -> 0%
where the time goes in v1:
time: 227 us
  Pallas kernels  222 us (98%)
  local copies, waits for them, and re-layouts  3.91 us (2%)
    pallas_call x1, Pallas kernels, on_device(): pl.pallas_call(functools.partial(kernel, nw, nn, width, depth), out_shape...  222 us

profile of v1, /device:TPU:16, one launch (start us, length us, event | category | flops | bytes accessed | tf_op | source)
XLA Modules:
  0.0 226.9 jit_solution(5929044256304757305)
XLA Ops:
  0.6 0.7 compare_select_fusion
  1.4 0.1 select_reduce_fusion
  1.5 221.5 %sketch.1 = (f32[512,256]{1,0:T(8,128)S(1)}, f32[128,4096]{1,0:T(8,128)}) custom-call(s32[512]{0:T(512)S(1)} %broadcast_add_fusion.slot_at, bf16[224,128,128]{2,1,0:T(8,128)(2,1)} %bitcast.2, bf16[512,2048]{1,0:T(8,128)(2,1)} %psi_hbm.1, bf16[4096,256]{1,0:T(8,128)(2,1)} %omega_hbm.1), custom_call_target="tpu_custom_call" | custom-call | tf_op jit(solution)/shard_map/sketch/pallas_call | solution.py:230
  223.0 0.8 copy.10
  223.8 3.1 %copy.11 = f32[128,4096]{1,0:T(8,128)} copy(f32[128,4096]{1,0:T(8,128)} %get-tuple-element.5) | data formatting | bytes 4194304
  (2 shorter events, 0.0 us)

commit v2 on v1

--- a/solution.py
+++ b/solution.py
@@ -13,7 +13,7 @@
 
 
 def kernel(
-    nw, nn, width, depth,
+    nw, nn, width, depth, tall, window, lag, late,
     slot_at, tiles_hbm, psi_hbm, omega_hbm, range_hbm, corange_hbm,
     tiles, psi, omega, dense, part, arrived, rpart, rarrived,
     in_sem, send_sem, recv_sem, rsend_sem, rrecv_sem, out_sem, rout_sem,
@@ -80,6 +80,44 @@
         at = pl.ds(pl.multiple_of(j * share, share), share)
         part[c, at, :] = part[c, at, :] + arrived[slot, c]
 
+    def await_sent(k, left):
+        s, c = k // chunks, k % chunks
+        j = s if left else nw - 1 - s
+        pltpu.make_async_copy(own(j, c), own(j, c), send_sem.at[j, c]).wait()
+
+    def make_room(k, left=False):
+        @pl.when(k >= chunks)
+        def _():
+            await_sent(k - window, left)
+
+    pieces = (nw - 1) * chunks
+
+    def line_step(k, carry):
+        nearer = 2 * me < nw
+        k_right = jnp.where(nearer, k, k - late)
+        k_left = jnp.where(nearer, k - late, k)
+
+        def forward(k, left):
+            within = jnp.logical_and(k >= 0, k < pieces)
+            s, c = jnp.maximum(k, 0) // chunks, jnp.maximum(k, 0) % chunks
+            share_at = s if left else nw - 1 - s
+            passes = me > share_at if left else me < share_at
+            inner = me < nw - 1 if left else me > 0
+
+            @pl.when(within & passes & (inner | (s > 0)))
+            def _():
+                @pl.when(inner)
+                def _():
+                    await_arrival(share_at, c)
+                    add_arrived(share_at, share_at, c)
+
+                make_room(k, left)
+                (leftward if left else rightward)(share_at, c).start()
+
+        forward(k_right, False)
+        forward(k_left, True)
+        return carry
+
     in_copies[0].wait()
     in_copies[1].wait()
     in_copies[2].wait()
@@ -109,14 +147,18 @@
         def _():
             leftward(0, c).start()
 
+        @pl.when(c >= lag)
+        def _():
+            line_step(c - lag, 0)
+
         chosen = omega[pl.ds(pl.multiple_of(c * width, width), width), :]
 
         def range_rows(m, carry):
-            at = pl.ds(pl.multiple_of(m * depth, depth), depth)
+            at = pl.ds(pl.multiple_of(m * tall, tall), tall)
             rpart[at, :] = rpart[at, :] + jnp.dot(dense[at, :], chosen, preferred_element_type=F32)
             return carry
 
-        lax.fori_loop(0, rows // depth, range_rows, 0)
+        lax.fori_loop(0, rows // tall, range_rows, 0)
         return carry
 
     lax.fori_loop(0, chunks, chunk_step, 0)
@@ -133,32 +175,7 @@
     for d in range(1, nn):
         range_copy(d).start()
 
-    def line_step(k, carry):
-        s, c = k // chunks, k % chunks
-        right_share = nw - 1 - s
-        left_share = s
-
-        @pl.when(jnp.logical_and(me < right_share, jnp.logical_or(me > 0, s > 0)))
-        def _():
-            @pl.when(me > 0)
-            def _():
-                await_arrival(right_share, c)
-                add_arrived(right_share, right_share, c)
-
-            rightward(right_share, c).start()
-
-        @pl.when(jnp.logical_and(me > left_share, jnp.logical_or(me < nw - 1, s > 0)))
-        def _():
-            @pl.when(me < nw - 1)
-            def _():
-                await_arrival(left_share, c)
-                add_arrived(left_share, left_share, c)
-
-            leftward(left_share, c).start()
-
-        return carry
-
-    lax.fori_loop(0, (nw - 1) * chunks, line_step, 0)
+    lax.fori_loop(chunks - lag, pieces + late, line_step, 0)
 
     at = pl.ds(pl.multiple_of(mine * rblock, rblock), rblock)
     for d in range(1, nn):
@@ -192,15 +209,17 @@
     lax.fori_loop(0, chunks, finish, 0)
 
     def drain(k, carry):
-        j, c = k // chunks, k % chunks
-
-        @pl.when(j != me)
-        def _():
-            pltpu.make_async_copy(own(j, c), own(j, c), send_sem.at[j, c]).wait()
-
-        return carry
-
-    lax.fori_loop(0, nw * chunks, drain, 0)
+        for left, sent in ((False, (nw - 1 - me) * chunks), (True, me * chunks)):
+            last = jnp.logical_and(k >= sent - window, k < sent)
+            first = jnp.logical_and(k < chunks - window, k < sent)
+
+            @pl.when(jnp.logical_or(first, last))
+            def _():
+                await_sent(k, left)
+
+        return carry
+
+    lax.fori_loop(0, (nw - 1) * chunks, drain, 0)
 
     def drain_out(c, carry):
         share_out(c).wait()
@@ -217,8 +236,12 @@
     rank, corank = omega.shape[1], psi.shape[0]
     rows, cols = psi.shape[1], omega.shape[0]
     row_blocks, col_blocks = rows // tile, cols // tile
-    width = 2 * tile
+    width = 4 * tile
     depth = 2 * tile
+    tall = rows // 2
+    window = 4
+    lag = 1
+    late = 2
     chunks = cols // width
     share, rblock = corank // nw, rows // nn
 
@@ -228,7 +251,7 @@
     slot_at = slots + jnp.sum(jnp.where(hit, back[None, :], 0), axis=1, dtype=jnp.int32)
 
     return pl.pallas_call(
-        functools.partial(kernel, nw, nn, width, depth),
+        functools.partial(kernel, nw, nn, width, depth, tall, window, lag, late),
         out_shape=(
             jax.ShapeDtypeStruct((rblock, rank), F32),
             jax.ShapeDtypeStruct((share, cols), F32),

time: 227 us -> 151 us (0.67)
  Pallas kernels: 222 us -> 146 us
    pallas_call x1, Pallas kernels: 222 us -> 146 us  [on_device(): pl.pallas_call(functools.partial(kernel, nw, nn, width, depth, tall, wind...]
where the time goes in v2:
time: 151 us
  Pallas kernels  146 us (97%)
  local copies, waits for them, and re-layouts  3.91 us (3%)
    pallas_call x1, Pallas kernels, on_device(): pl.pallas_call(functools.partial(kernel, nw, nn, width, depth, tall, wind...  146 us
    unnamed x2, local copies, waits for them, and re-layouts  3.91 us

profile of v2, /device:TPU:16, one launch (start us, length us, event | category | flops | bytes accessed | tf_op | source)
XLA Modules:
  0.0 151.2 jit_solution(10508413115549655010)
XLA Ops:
  0.6 0.7 compare_select_fusion
  1.4 0.1 select_reduce_fusion
  1.5 145.8 %sketch.1 = (f32[512,256]{1,0:T(8,128)S(1)}, f32[128,4096]{1,0:T(8,128)}) custom-call(s32[512]{0:T(512)S(1)} %broadcast_add_fusion.slot_at, bf16[224,128,128]{2,1,0:T(8,128)(2,1)} %bitcast.2, bf16[512,2048]{1,0:T(8,128)(2,1)} %psi_hbm.1, bf16[4096,256]{1,0:T(8,128)(2,1)} %omega_hbm.1), custom_call_target="tpu_custom_call" | custom-call | tf_op jit(solution)/shard_map/sketch/pallas_call | solution.py:253
  147.3 0.8 copy.10
  148.1 3.1 %copy.11 = f32[128,4096]{1,0:T(8,128)} copy(f32[128,4096]{1,0:T(8,128)} %get-tuple-element.5) | data formatting | bytes 4194304
  (2 shorter events, 0.0 us)

commit v3 on v2

--- a/solution.py
+++ b/solution.py
@@ -119,8 +119,6 @@
         return carry
 
     in_copies[0].wait()
-    in_copies[1].wait()
-    in_copies[2].wait()
 
     def chunk_step(c, carry):
         def place(r, carry):
@@ -132,6 +130,10 @@
 
         lax.fori_loop(0, row_blocks, place, 0)
 
+        @pl.when(c == 0)
+        def _():
+            in_copies[1].wait()
+
         def corange_rows(m, carry):
             at = pl.ds(pl.multiple_of(m * depth, depth), depth)
             part[c, at, :] = jnp.dot(psi[at, :], dense[...], preferred_element_type=F32)
@@ -150,6 +152,10 @@
         @pl.when(c >= lag)
         def _():
             line_step(c - lag, 0)
+
+        @pl.when(c == 0)
+        def _():
+            in_copies[2].wait()
 
         chosen = omega[pl.ds(pl.multiple_of(c * width, width), width), :]
 
@@ -254,10 +260,10 @@
         functools.partial(kernel, nw, nn, width, depth, tall, window, lag, late),
         out_shape=(
             jax.ShapeDtypeStruct((rblock, rank), F32),
-            jax.ShapeDtypeStruct((share, cols), F32),
+            pltpu.VMEM((share, cols), F32),
         ),
         in_specs=[pl.BlockSpec(memory_space=pltpu.SMEM)] + [pl.BlockSpec(memory_space=pl.ANY)] * 3,
-        out_specs=(pl.BlockSpec(memory_space=pl.ANY),) * 2,
+        out_specs=(pl.BlockSpec(memory_space=pl.ANY), pl.BlockSpec(memory_space=pltpu.VMEM)),
         scratch_shapes=[
             pltpu.VMEM((slots + 1, tile, tile), BF16),
             pltpu.VMEM((corank, rows), BF16),

time: 151 us -> 149 us (0.987)
  local copies, waits for them, and re-layouts: 3.91 us -> 2.16 us
    unnamed x2 -> x4, local copies, waits for them, and re-layouts: 3.91 us -> 2.16 us
where the time goes in v3:
time: 149 us
  Pallas kernels  145 us (97%)
  local copies, waits for them, and re-layouts  2.16 us (1%)
    pallas_call x1, Pallas kernels, on_device(): pl.pallas_call(functools.partial(kernel, nw, nn, width, depth, tall, wind...  145 us

profile of v3, /device:TPU:16, one launch (start us, length us, event | category | flops | bytes accessed | tf_op | source)
XLA Modules:
  0.0 148.9 jit_solution(2398298303127635185)
XLA Ops:
  0.6 0.7 compare_select_fusion
  1.4 0.1 select_reduce_fusion
  1.5 0.6 broadcast_add_fusion.slot_at
  2.1 144.6 %sketch.1 = (f32[512,256]{1,0:T(8,128)}, f32[128,4096]{1,0:T(8,128)S(1)}) custom-call(s32[512]{0:T(512)} %broadcast_add_fusion.slot_at, bf16[224,128,128]{2,1,0:T(8,128)(2,1)} %bitcast.2, bf16[512,2048]{1,0:T(8,128)(2,1)} %psi_hbm.1, bf16[4096,256]{1,0:T(8,128)(2,1)} %omega_hbm.1), custom_call_target="tpu_custom_call" | custom-call | tf_op jit(solution)/shard_map/sketch/pallas_call | solution.py:259
  146.7 0.0 copy-start
  146.7 1.3 copy.10
  148.0 0.0 copy-done
  148.1 0.8 copy.11
  (1 shorter events, 0.0 us)
Async XLA Ops:
  146.7 1.4 copy-start
